TPU v7x, 32 devices: a whole 2x2x4 slice. The times are simulated.
32 devices in a mesh: row: 4 (over y, x), col: 8 (over z, core).
Axes of the slice: x: 2, y: 2, z: 4, core: 2. Of those that a mesh axis runs over, the one named last changes fastest.
Arguments:
- tokens: bfloat16 [48, 96, 768], P('row', 'col'), may hold values from -6 to 6
- w_in: bfloat16 [768, 1536], replicated, may hold values from -0.21875 to 0.21875
- w_xproj: bfloat16 [768, 80], replicated, may hold values from -0.21875 to 0.21875
- w_dt: bfloat16 [48, 768], replicated, may hold values from -0.875 to 0.875
- dt_bias: float32 [768], replicated, may hold values from -7 to -2.3
- a_log: float32 [16, 768], replicated, may hold values from 0 to 2.77
- d_skip: float32 [768], replicated, may hold values from 0.5 to 1.5
- w_out: bfloat16 [768, 768], replicated, may hold values from -0.21875 to 0.21875
- out_grad: bfloat16 [48, 96, 768], P('row', 'col'), may hold values from -6 to 6
Outputs:
- layer_out: bfloat16 [48, 96, 768], P('row', 'col')
- token_grad: bfloat16 [48, 96, 768], P('row', 'col')
All inputs are finite; a program needn't handle non-finite values.
Results may differ from a plain program's by a relative error of at most 0.0064.
Values sent between devices are 32-bit elements; how exact they have to be, the bound alone decides.
A program may use at most 192 MiB of HBM per device.

v0:
```python
import functools
import math

import jax
import jax.numpy as jnp
from jax import lax
from jax.experimental import pallas as pl
from jax.experimental.pallas import tpu as pltpu
from jax.sharding import PartitionSpec as P

MESH = pl.DeviceIdType.MESH
LANES = 128
F32 = jnp.float32


def silu_grad(values):
    sigmoid = jax.nn.sigmoid(values)
    return sigmoid * (1.0 + values * (1.0 - sigmoid))


def dot_transposed(left, right):
    return lax.dot_general(
        left, right, (((1,), (1,)), ((), ())), preferred_element_type=jnp.float32
    )


def scan_kernel(
    sizes,
    step_ref, u_ref, g_ref, rate_ref, b_ref, c_ref, rsum_ref, csum_ref,
    out_ref, rb_ref, sd_ref, bacc_ref, cacc_ref,
    decay, rows, cols, prow, pcol,
    e1r, e1c, e2r, e2c, in1r, in1c, in2r, in2c, fcar,
    send_sem, recv_sem,
):
    n_row, n_col, tr, tc, chunks, states = sizes
    r = lax.axis_index("row")
    p = lax.axis_index("col")
    left, right = (r, lax.rem(p + n_col - 1, n_col)), (r, lax.rem(p + 1, n_col))
    up, down = (lax.rem(r + n_row - 1, n_row), p), (lax.rem(r + 1, n_row), p)
    first_col, last_col = p == 0, p == n_col - 1
    first_row, last_row = r == 0, r == n_row - 1

    barrier = pltpu.get_barrier_semaphore()
    edges = ((first_col, left), (last_col, right), (first_row, up), (last_row, down))
    for edge, neighbour in edges:
        @pl.when(jnp.logical_not(edge))
        def _():
            pl.semaphore_signal(barrier, inc=1, device_id=neighbour, device_id_type=MESH)
    peers = sum(jnp.where(edge, 0, 1) for edge, _ in edges)
    pl.semaphore_wait(barrier, peers)

    links = (
        (e1r, in1r, right, first_col, last_col, prow),
        (e1c, in1c, up, last_row, first_row, pcol),
        (e2c, in2c, down, first_row, last_row, pcol),
        (e2r, in2r, left, last_col, first_col, prow),
    )

    def copy(kind, k):
        source, target, where = links[kind][:3]
        return pltpu.make_async_remote_copy(
            src_ref=source.at[k],
            dst_ref=target.at[k],
            send_sem=send_sem.at[kind, k],
            recv_sem=recv_sem.at[kind, k],
            device_id=where,
            device_id_type=MESH,
        )

    for kind in range(4):
        @pl.when(links[kind][3])
        def _():
            links[kind][1][...] = jnp.zeros_like(links[kind][1])

    def head_send(kind, k):
        head, tail = links[kind][3:5]

        @pl.when(jnp.logical_and(head, jnp.logical_not(tail)))
        def _():
            copy(kind, k).start()

    def forward(kind, k):
        source, target, _, head, tail, product = links[kind]

        @pl.when(jnp.logical_not(head))
        def _():
            copy(kind, k).wait_recv()

        @pl.when(jnp.logical_not(jnp.logical_or(head, tail)))
        def _():
            source[k] = source[k] + product[k] * target[k]
            copy(kind, k).start()

    def lanes(k):
        return pl.ds(pl.multiple_of(k * LANES, LANES), LANES)

    zero = jnp.zeros((states, LANES), F32)

    @pl.loop(0, chunks)
    def _(k):
        cut = lanes(k)
        rate = rate_ref[:, cut]
        for i in range(tr):
            prow[k, i] = jnp.exp2(rate * rsum_ref[i : i + 1, cut])
        for j in range(tc):
            pcol[k, j] = jnp.exp2(rate * csum_ref[j : j + 1, cut])

        def line(count, terms):
            i = tr - 1 - count
            state = zero
            after = []
            for j in range(tc):
                t = i * tc + j
                d = jnp.exp2(rate * step_ref[i, j : j + 1, cut])
                decay[k, t] = d
                state = d * state + u_ref[i, j : j + 1, cut] * b_ref[t]
                after.append(d * (terms[j] + g_ref[i, j : j + 1, cut] * c_ref[t]))
            e1r[k, i] = state
            return tuple(after)

        terms = lax.fori_loop(0, tr, line, (zero,) * tc)
        for j in range(tc):
            e1c[k, j] = terms[j]
        head_send(0, k)
        head_send(1, k)

    @pl.loop(0, chunks)
    def _(k):
        cut = lanes(k)
        forward(0, k)
        forward(1, k)

        def down_line(i, states_in):
            state = in1r[k, i]
            after = []
            for j in range(tc):
                t = i * tc + j
                d = decay[k, t]
                state = d * state + u_ref[i, j : j + 1, cut] * b_ref[t]
                rows[k, t] = state
                after.append(d * states_in[j] + state)
            return tuple(after)

        ends = lax.fori_loop(0, tr, down_line, (zero,) * tc)
        for j in range(tc):
            e2c[k, j] = ends[j]
        head_send(2, k)

        def up_line(count, terms):
            i = tr - 1 - count
            term = zero
            after = [None] * tc
            for j in reversed(range(tc)):
                t = i * tc + j
                d = decay[k, t]
                adjoint = terms[j] + g_ref[i, j : j + 1, cut] * c_ref[t]
                cols[k, t] = adjoint
                after[j] = d * adjoint
                term = d * (adjoint + term)
            e2r[k, i] = term
            return tuple(after)

        lax.fori_loop(0, tr, up_line, tuple(in1c[k, j] for j in range(tc)))
        head_send(3, k)

    bacc_ref[...] = jnp.zeros_like(bacc_ref)
    cacc_ref[...] = jnp.zeros_like(cacc_ref)

    @pl.loop(0, chunks)
    def _(k):
        cut = lanes(k)
        rate = rate_ref[:, cut]
        forward(2, k)
        forward(3, k)
        for j in range(tc):
            fcar[j] = in2c[k, j]

        def last_line(i, carry):
            term = in2r[k, i]
            for j in reversed(range(tc)):
                t = i * tc + j
                d = decay[k, t]
                adjoint = cols[k, t]
                state = rows[k, t]
                before = in1r[k, i] if j == 0 else rows[k, t - 1]
                passed = d * fcar[j]
                full = passed + state
                fcar[j] = full
                total = adjoint + term
                term = d * total
                slope = adjoint * passed + term * before
                sd_ref[i, j : j + 1, cut] = jnp.sum(slope * rate, axis=0, keepdims=True)
                rb_ref[i, j : j + 1, cut] = jnp.sum(total * b_ref[t], axis=0, keepdims=True)
                out_ref[i, j : j + 1, cut] = jnp.sum(full * c_ref[t], axis=0, keepdims=True)
                bacc_ref[t] += total * u_ref[i, j : j + 1, cut]
                cacc_ref[t] += full * g_ref[i, j : j + 1, cut]
            return carry

        lax.fori_loop(0, tr, last_line, 0)

    for kind in range(4):
        tail = links[kind][4]

        @pl.when(jnp.logical_not(tail))
        def _():
            @pl.loop(0, chunks)
            def _(k):
                copy(kind, k).wait_send()


def scans(mesh_shape, tr, tc, step, u, g, rate, b_wide, c_wide, rsum, csum):
    cells, width = tr * tc, step.shape[-1]
    states = rate.shape[0]
    chunks = width // LANES
    sizes = (mesh_shape["row"], mesh_shape["col"], tr, tc, chunks, states)
    grid_buf = pltpu.VMEM((chunks, cells, states, LANES), F32)
    row_buf = pltpu.VMEM((chunks, tr, states, LANES), F32)
    col_buf = pltpu.VMEM((chunks, tc, states, LANES), F32)
    wide = jax.ShapeDtypeStruct((tr, tc, width), F32)
    acc = jax.ShapeDtypeStruct((cells, states, LANES), F32)
    return pl.pallas_call(
        functools.partial(scan_kernel, sizes),
        out_shape=(wide, wide, wide, acc, acc),
        in_specs=[pl.BlockSpec(memory_space=pltpu.VMEM)] * 8,
        out_specs=(pl.BlockSpec(memory_space=pltpu.VMEM),) * 5,
        scratch_shapes=[
            grid_buf, grid_buf, grid_buf, row_buf, col_buf,
            row_buf, col_buf, row_buf, col_buf, row_buf, col_buf, row_buf, col_buf,
            pltpu.VMEM((tc, states, LANES), F32),
            pltpu.SemaphoreType.DMA((4, chunks)),
            pltpu.SemaphoreType.DMA((4, chunks)),
        ],
        compiler_params=pltpu.CompilerParams(
            collective_id=0, has_side_effects=True, vmem_limit_bytes=56 * 1024 * 1024
        ),
    )(step, u, g, rate, b_wide, c_wide, rsum, csum)


def body(mesh_shape, tokens, w_in, w_xproj, w_dt, dt_bias, a_log, d_skip, w_out, out_grad):
    tile_rows, tile_cols, model_width = tokens.shape
    cell_count = tile_rows * tile_cols
    low_rank, inner_width = w_dt.shape
    states = a_log.shape[0]
    flat_tokens = tokens.reshape(cell_count, model_width)
    projected = jnp.dot(flat_tokens, w_in, preferred_element_type=jnp.float32)
    x_pre = projected[:, :inner_width]
    z_pre = projected[:, inner_width:]
    x_act = jax.nn.silu(x_pre).astype(jnp.bfloat16)
    x_dbl = jnp.dot(x_act, w_xproj, preferred_element_type=jnp.float32)
    dt_low = x_dbl[:, :low_rank].astype(jnp.bfloat16)
    b_sel = x_dbl[:, low_rank : low_rank + states]
    c_sel = x_dbl[:, low_rank + states :]
    dt_pre = jnp.dot(dt_low, w_dt, preferred_element_type=jnp.float32) + dt_bias
    step_size = jax.nn.softplus(dt_pre)
    gated_grad = dot_transposed(out_grad.reshape(cell_count, model_width), w_out)
    z_silu = jax.nn.silu(z_pre)
    scan_grad = gated_grad * z_silu
    x_wide = x_act.astype(F32)
    step_grid = step_size.reshape(tile_rows, tile_cols, inner_width)
    shape = (cell_count, states, LANES)
    grid = (tile_rows, tile_cols, inner_width)
    cf, rb, slope, bacc, cacc = scans(
        mesh_shape, tile_rows, tile_cols,
        step_grid, (step_size * x_wide).reshape(grid), scan_grad.reshape(grid), -jnp.exp(a_log) * math.log2(math.e),
        jnp.broadcast_to(b_sel[:, :, None], shape), jnp.broadcast_to(c_sel[:, :, None], shape),
        jnp.sum(step_grid, axis=1), jnp.sum(step_grid, axis=0),
    )
    cf, rb, slope = (a.reshape(cell_count, inner_width) for a in (cf, rb, slope))
    scan_out = cf + d_skip * x_wide
    step_grad = slope * math.log(2.0) + rb * x_wide
    xscan_grad = rb * step_size + scan_grad * d_skip
    gated_out = (scan_out * z_silu).astype(jnp.bfloat16)
    layer_out = jnp.dot(gated_out, w_out, preferred_element_type=jnp.float32).astype(jnp.bfloat16)
    z_grad = gated_grad * scan_out * silu_grad(z_pre)
    pre_grad = (step_grad * jax.nn.sigmoid(dt_pre)).astype(jnp.bfloat16)
    low_grad = dot_transposed(pre_grad, w_dt)
    dbl_grad = jnp.concatenate(
        [low_grad, jnp.sum(bacc, axis=2), jnp.sum(cacc, axis=2)], axis=1
    ).astype(jnp.bfloat16)
    x_grad = xscan_grad + dot_transposed(dbl_grad, w_xproj)
    proj_grad = jnp.concatenate([x_grad * silu_grad(x_pre), z_grad], axis=1).astype(jnp.bfloat16)
    token_grad = dot_transposed(proj_grad, w_in).astype(jnp.bfloat16)
    return (
        layer_out.reshape(tile_rows, tile_cols, model_width),
        token_grad.reshape(tile_rows, tile_cols, model_width),
    )


def solution(mesh):
    return jax.shard_map(
        functools.partial(body, dict(mesh.shape)),
        mesh=mesh,
        in_specs=(P("row", "col", None), P(), P(), P(), P(), P(), P(), P(), P("row", "col", None)),
        out_specs=(P("row", "col", None), P("row", "col", None)),
        check_vma=False,
    )
```

profile of v0, /device:TPU:6, one launch (start us, length us, event | category | flops | bytes accessed | tf_op | source)
XLA Modules:
  0.0 104.2 jit_solution(10617479112839045932)
XLA Ops:
  0.6 1.6 %negate_multiply_fusion.rate_ref = f32[16,768]{1,0:T(8,128)} fusion(f32[16,768]{1,0:T(8,128)} %param.14), kind=kLoop, calls=%fused_computation.28 | loop fusion | flops 24576 | bytes 98304 | tf_op jit(solution)/shard_map/mul | solution.py:264
  2.2 1.0 reshape.38
  3.2 1.0 reshape.41
  4.3 0.5 fusion.25
  4.8 0.7 copy-done.18
  5.6 1.3 %fusion.13 = (f32[144,768]{1,0:T(8,128)S(1)}, bf16[144,768]{1,0:T(8,128)(2,1)S(1)}, f32[144,768]{1,0:T(8,128)}) fusion(f32[144,1536]{1,0:T(8,128)S(1)} %fusion.25, bf16[144,768]{1,0:T(8,128)(2,1)S(1)} %reshape.41, bf16[768,768]{1,0:T(8,128)(2,1)S(1)} %copy-done.18), kind=kOutput, calls=%fused_computation.27 | convolution fusion | flops 170975232 | bytes 3391488 | tf_op jit(solution)/shard_map/dot_general | solution.py:22
  6.9 0.2 fusion.26
  7.1 0.1 fusion.24
  7.2 0.9 reshape.42.g_ref
  8.1 1.4 %broadcast_in_dim.5.c_ref = f32[144,16,128]{2,1,0:T(8,128)} broadcast(f32[144,16]{1,0:T(8,128)S(1)} %get-tuple-element.18), dimensions={0,1} | broadcast | bytes 1188864 | tf_op jit(solution)/shard_map/broadcast_in_dim | solution.py:265
  9.5 1.4 %broadcast_in_dim.4.b_ref = f32[144,16,128]{2,1,0:T(8,128)} broadcast(f32[144,16]{1,0:T(8,128)S(1)} %get-tuple-element.19), dimensions={0,1} | broadcast | bytes 1188864 | tf_op jit(solution)/shard_map/broadcast_in_dim | solution.py:265
  10.9 1.4 %convert_multiply_fusion.2 = (f32[144,768]{1,0:T(8,128)S(1)}, f32[144,768]{1,0:T(8,128)}, f32[144,768]{1,0:T(8,128)}) fusion(bf16[144,768]{1,0:T(8,128)(2,1)S(1)} %get-tuple-element.15, f32[768]{0:T(1024)S(1)} %copy-done.16, bf16[48,768]{1,0:T(8,128)(2,1)S(1)} %copy-done.15, f32[144,80]{1,0:T(8,128)S(1)} %fusion.26), kind=kOutput, calls=%fused_computation.10 | convolution fusion | flops 11612160 | bytes 1662976 | tf_op jit(solution)/shard_map/dot_general | solution.py:253
  12.3 0.9 reshape.40.u_ref
  13.2 1.1 %reshape.39.step_ref = f32[12,12,768]{2,1,0:T(8,128)S(1)} reshape(f32[144,768]{1,0:T(8,128)} %get-tuple-element.17) | data formatting | bytes 884736 | tf_op jit(solution)/shard_map/reshape | solution.py:259
  14.2 0.8 fusion.23
  15.0 0.1 copy-done.1
  15.1 72.2 %shard_map.104 = (f32[12,12,768]{2,1,0:T(8,128)}, f32[12,12,768]{2,1,0:T(8,128)}, f32[12,12,768]{2,1,0:T(8,128)}, f32[144,16,128]{2,1,0:T(8,128)}, f32[144,16,128]{2,1,0:T(8,128)}) custom-call(f32[12,12,768]{2,1,0:T(8,128)} %copy-done.1, f32[12,12,768]{2,1,0:T(8,128)} %reshape.40.u_ref, f32[12,12,768]{2,1,0:T(8,128)} %reshape.42.g_ref, ...), custom_call_target="tpu_custom_call" | custom-call | tf_op jit(solution)/shard_map/pallas_call | solution.py:221
  87.4 2.0 %reshape.43 = f32[144,768]{1,0:T(8,128)} reshape(f32[12,12,768]{2,1,0:T(8,128)} %get-tuple-element.7) | data formatting | bytes 884736 | tf_op jit(solution)/shard_map/reshape | solution.py:268
  89.4 2.2 %multiply_convert_fusion = bf16[144,768]{1,0:T(8,128)(2,1)} fusion(f32[144,768]{1,0:T(8,128)} %get-tuple-element.20, f32[144,1536]{1,0:T(8,128)S(1)} %copy-done.3, f32[144,768]{1,0:T(8,128)} %reshape.43, bf16[144,768]{1,0:T(8,128)(2,1)S(1)} %get-tuple-element.15, f32[768]{0:T(1024)S(1)} %copy-done.17), kind=kLoop, calls=%fused_computation.18 | loop fusion | flops 1437696 | bytes 1772544 | tf_op jit(solution)/shard_map/convert.1
  91.6 1.1 %convolution_convert_fusion = bf16[144,768]{1,0:T(8,128)(2,1)} fusion(bf16[768,768]{1,0:T(8,128)(2,1)S(1)} %copy-done.19, f32[144,768]{1,0:T(8,128)S(1)} %copy-done.5, bf16[144,768]{1,0:T(8,128)(2,1)S(1)} %get-tuple-element.15, f32[768]{0:T(1024)S(1)} %copy-done.17, f32[144,1536]{1,0:T(8,128)S(1)} %copy-done.3), kind=kOutput, calls=%fused_computation.4 | convolution fusion | flops 170975232 | bytes 2510848 | tf_op jit(solution)/shard_map/dot_general | solution.py:273
  92.7 1.7 %reduce_sum.38 = bf16[144,16]{1,0:T(8,128)(2,1)S(1)} reduce(f32[144,16,128]{2,1,0:T(8,128)} %get-tuple-element.10, f32[]{:T(128)} %constant.3.clone.1), dimensions={2}, to_apply=%region_2.3 | reduce | flops 292608 | bytes 1184260 | tf_op jit(solution)/shard_map/reduce_sum | solution.py:278
  94.4 1.7 %reduce_sum.39 = bf16[144,16]{1,0:T(8,128)(2,1)S(1)} reduce(f32[144,16,128]{2,1,0:T(8,128)} %get-tuple-element.11, f32[]{:T(128)} %constant.3.clone.1), dimensions={2}, to_apply=%region_3.4 | reduce | flops 292608 | bytes 1184260 | tf_op jit(solution)/shard_map/reduce_sum | solution.py:278
  96.1 0.8 reshape.44
  96.8 0.8 reshape.45
  97.7 1.1 %broadcast_multiply_fusion = f32[12,12,768]{2,1,0:T(8,128)S(1)} fusion(f32[12,12,768]{2,1,0:T(8,128)} %get-tuple-element.9), kind=kLoop, calls=%fused_computation.24 | loop fusion | flops 110592 | bytes 884736 | tf_op jit(solution)/shard_map/mul | solution.py:270
  98.8 0.8 mul.88
  99.6 1.7 %convolution_convert_fusion.2 = bf16[144,48]{1,0:T(8,128)(2,1)S(1)} fusion(bf16[48,768]{1,0:T(8,128)(2,1)S(1)} %copy-done.15, f32[144,768]{1,0:T(8,128)} %mul.88, f32[144,768]{1,0:T(8,128)} %reshape.45, bf16[144,768]{1,0:T(8,128)(2,1)S(1)} %get-tuple-element.15, f32[144,768]{1,0:T(8,128)} %get-tuple-element.21), kind=kOutput, calls=%fused_computation.7 | convolution fusion | flops 11508480 | bytes 1635840 | tf_op jit(solution)/shard_map/dot_general | solution.py:22
  101.4 0.1 copy-done.10
  101.6 0.6 fusion.1
  102.1 0.4 copy-done.11
  102.5 0.9 convolution_convert_fusion.1
  103.4 0.8 reshape.46
  (36 shorter events, 0.2 us)
Async XLA Ops:
  0.6 3.6 %copy-start = (bf16[768,1536]{1,0:T(8,128)(2,1)S(1)}, bf16[768,1536]{1,0:T(8,128)(2,1)}, u32[]{:S(2)}) copy-start(bf16[768,1536]{1,0:T(8,128)(2,1)} %param.10) | copy-start | bytes 7077892
  4.3 1.3 %copy-start.18 = (bf16[768,768]{1,0:T(8,128)(2,1)S(1)}, bf16[768,768]{1,0:T(8,128)(2,1)}, u32[]{:S(2)}) copy-start(bf16[768,768]{1,0:T(8,128)(2,1)} %param.16) | copy-start | bytes 3538948
  5.5 1.4 %copy-start.2 = (f32[144,1536]{1,0:T(8,128)}, f32[144,1536]{1,0:T(8,128)S(1)}, u32[]{:S(2)}) copy-start(f32[144,1536]{1,0:T(8,128)S(1)} %fusion.25) | copy-start | bytes 2654212
  5.5 1.4 %copy-start.13 = (bf16[768,80]{0,1:T(8,128)(2,1)S(1)}, bf16[768,80]{0,1:T(8,128)(2,1)}, u32[]{:S(2)}) copy-start(bf16[768,80]{0,1:T(8,128)(2,1)} %param.11) | copy-start | bytes 368644
  6.9 2.6 %copy-start.8 = (f32[144,768]{1,0:T(8,128)}, f32[144,768]{1,0:T(8,128)S(1)}, u32[]{:S(2)}) copy-start(f32[144,768]{1,0:T(8,128)S(1)} %get-tuple-element.14) | copy-start | bytes 1327108
  8.1 2.8 %copy-start.15 = (bf16[48,768]{1,0:T(8,128)(2,1)S(1)}, bf16[48,768]{1,0:T(8,128)(2,1)}, u32[]{:S(2)}) copy-start(bf16[48,768]{1,0:T(8,128)(2,1)} %param.12) | copy-start | bytes 221188
  8.1 2.8 %copy-start.16 = (f32[768]{0:T(1024)S(1)}, f32[768]{0:T(1024)}, u32[]{:S(2)}) copy-start(f32[768]{0:T(1024)} %param.13) | copy-start | bytes 9220
  14.2 0.9 copy-start.1
  15.1 74.2 %copy-start.17 = (f32[768]{0:T(1024)S(1)}, f32[768]{0:T(1024)}, u32[]{:S(2)}) copy-start(f32[768]{0:T(1024)} %param.15) | copy-start | bytes 9220
  87.4 2.0 %copy-start.3 = (f32[144,1536]{1,0:T(8,128)S(1)}, f32[144,1536]{1,0:T(8,128)}, u32[]{:S(2)}) copy-start(f32[144,1536]{1,0:T(8,128)} %copy-done.2) | copy-start | bytes 2654212
  89.4 2.2 %copy-start.5 = (f32[144,768]{1,0:T(8,128)S(1)}, f32[144,768]{1,0:T(8,128)}, u32[]{:S(2)}) copy-start(f32[144,768]{1,0:T(8,128)} %reshape.43) | copy-start | bytes 1327108
  89.4 2.2 %copy-start.19 = (bf16[768,768]{1,0:T(8,128)(2,1)S(1)}, bf16[768,768]{1,0:T(8,128)(2,1)}, u32[]{:S(2)}) copy-start(bf16[768,768]{1,0:T(8,128)(2,1)} %param.16) | copy-start | bytes 3538948
  92.7 3.4 %copy-start.12 = (bf16[144,768]{1,0:T(8,128)(2,1)S(1)}, bf16[144,768]{1,0:T(8,128)(2,1)}, u32[]{:S(2)}) copy-start(bf16[144,768]{1,0:T(8,128)(2,1)} %convolution_convert_fusion) | copy-start | bytes 663556
  92.7 4.2 %copy-start.6 = (f32[12,12,768]{2,1,0:T(8,128)S(1)}, f32[12,12,768]{2,1,0:T(8,128)}, u32[]{:S(2)}) copy-start(f32[12,12,768]{2,1,0:T(8,128)} %get-tuple-element.8) | copy-start | bytes 1327108
  99.6 1.7 %copy-start.4 = (f32[144,1536]{1,0:T(8,128)S(1)}, f32[144,1536]{1,0:T(8,128)}, u32[]{:S(2)}) copy-start(f32[144,1536]{1,0:T(8,128)} %copy-done.2) | copy-start | bytes 2654212
  99.6 1.7 %copy-start.7 = (f32[144,768]{1,0:T(8,128)S(1)}, f32[144,768]{1,0:T(8,128)}, u32[]{:S(2)}) copy-start(f32[144,768]{1,0:T(8,128)} %get-tuple-element.21) | copy-start | bytes 1327108
  99.6 1.8 %copy-start.9 = (f32[144,768]{1,0:T(8,128)S(1)}, f32[144,768]{1,0:T(8,128)}, u32[]{:S(2)}) copy-start(f32[144,768]{1,0:T(8,128)} %copy-done.8) | copy-start | bytes 1327108
  99.6 1.9 %copy-start.10 = (f32[144,768]{1,0:T(8,128)S(1)}, f32[144,768]{1,0:T(8,128)}, u32[]{:S(2)}) copy-start(f32[144,768]{1,0:T(8,128)} %reshape.45) | copy-start | bytes 1327108
  99.6 2.0 %copy-start.14 = (bf16[768,80]{0,1:T(8,128)(2,1)S(1)}, bf16[768,80]{0,1:T(8,128)(2,1)}, u32[]{:S(2)}) copy-start(bf16[768,80]{0,1:T(8,128)(2,1)} %param.11) | copy-start | bytes 368644
  101.6 0.9 copy-start.11
where the time goes:
time: 105 us; the launch traced here: 104 us
  Pallas kernels  72.2 us (69%)
  local copies, waits for them, and re-layouts  14.4 us (14%)
  other arithmetic  9.06 us (9%)
  matrix products  7.69 us (7%)
    pallas_call x1, Pallas kernels, scans(): pl.pallas_call(functools.partial(scan_kernel, sizes), out_shape=(wide, wi...  72.2 us
    dot_general x4, matrix products, dot_transposed(): lax.dot_general(left, right, (((1,), (1,)), ((), ())), preferred_element_...  4.49 us
    reshape x2, local copies, waits for them, and re-layouts, body(): a.reshape(cell_count, inner_width)  2.82 us
    another operation x1, other arithmetic  2.17 us

commit v1 on v0

v1 whole, which is shorter than its diff:
```python
import functools
import math

import jax
import jax.numpy as jnp
from jax import lax
from jax.experimental import pallas as pl
from jax.experimental.pallas import tpu as pltpu
from jax.sharding import PartitionSpec as P

MESH = pl.DeviceIdType.MESH
LANES = 128
BLOCK = 256
F32 = jnp.float32
BF16 = jnp.bfloat16


def sigmoid(values):
    return 1.0 / (1.0 + jnp.exp(-values))


def silu_grad(values):
    gate = sigmoid(values)
    return gate * (1.0 + values * (1.0 - gate))


def dot(left, right):
    return jnp.dot(left, right, preferred_element_type=F32)


def dot_transposed(left, right):
    return lax.dot_general(left, right, (((1,), (1,)), ((), ())), preferred_element_type=F32)


def layer_kernel(
    sizes,
    tokens_ref, w_in_ref, w_xproj_ref, w_dt_ref, bias_ref, a_log_ref, skip_ref, w_out_ref, grad_ref,
    layer_ref, token_grad_ref,
    pad_ref, x_pre_ref, z_pre_ref, x_ref, step_ref, u_ref, g_ref, gated_ref, dt_ref,
    out_ref, rb_ref, sd_ref, proj_ref, xd_ref, b_ref, c_ref, bacc_ref, cacc_ref,
    decay, rows, cols, prow, pcol,
    e1r, e1c, e2r, e2c, in1r, in1c, in2r, in2c, fcar,
    send_sem, recv_sem,
):
    n_row, n_col, tr, tc, chunks, states, rank = sizes
    pad = pad_ref.shape[1]
    cells = tr * pad
    width = x_ref.shape[-1]
    model = pad_ref.shape[-1]
    r = lax.axis_index("row")
    p = lax.axis_index("col")
    left, right = (r, lax.rem(p + n_col - 1, n_col)), (r, lax.rem(p + 1, n_col))
    up, down = (lax.rem(r + n_row - 1, n_row), p), (lax.rem(r + 1, n_row), p)
    first_col, last_col = p == 0, p == n_col - 1
    first_row, last_row = r == 0, r == n_row - 1

    barrier = pltpu.get_barrier_semaphore()
    edges = ((first_col, left), (last_col, right), (first_row, up), (last_row, down))
    for edge, neighbour in edges:
        @pl.when(jnp.logical_not(edge))
        def _():
            pl.semaphore_signal(barrier, inc=1, device_id=neighbour, device_id_type=MESH)
    peers = sum(jnp.where(edge, 0, 1) for edge, _ in edges)
    pl.semaphore_wait(barrier, peers)

    links = (
        (e1r, in1r, right, first_col, last_col, prow),
        (e1c, in1c, up, last_row, first_row, pcol),
        (e2c, in2c, down, first_row, last_row, pcol),
        (e2r, in2r, left, last_col, first_col, prow),
    )

    def copy(kind, k):
        source, target, where = links[kind][:3]
        return pltpu.make_async_remote_copy(
            src_ref=source.at[k],
            dst_ref=target.at[k],
            send_sem=send_sem.at[kind, k],
            recv_sem=recv_sem.at[kind, k],
            device_id=where,
            device_id_type=MESH,
        )

    for kind in range(4):
        @pl.when(links[kind][3])
        def _():
            links[kind][1][...] = jnp.zeros_like(links[kind][1])

    def head_send(kind, k):
        head, tail = links[kind][3:5]

        @pl.when(jnp.logical_and(head, jnp.logical_not(tail)))
        def _():
            copy(kind, k).start()

    def forward(kind, k):
        source, target, _, head, tail, product = links[kind]

        @pl.when(jnp.logical_not(head))
        def _():
            copy(kind, k).wait_recv()

        @pl.when(jnp.logical_not(jnp.logical_or(head, tail)))
        def _():
            source[k] = source[k] + product[k] * target[k]
            copy(kind, k).start()

    def rates(cut):
        return jnp.exp(a_log_ref[:, cut]) * -math.log2(math.e)

    def lanes(k):
        return pl.ds(pl.multiple_of(k * LANES, LANES), LANES)

    def flat(ref):
        return ref[...].reshape(cells, ref.shape[-1])

    def put(ref, cut, values):
        ref[:, :, cut] = values.reshape(tr, pad, values.shape[-1])

    def get(ref, cut):
        values = ref[:, :, cut]
        return values.reshape(cells, values.shape[-1])

    blocks = [slice(at, at + BLOCK) for at in range(0, width, BLOCK)]
    pad_ref[:, tc:, :] = jnp.zeros((tr, pad - tc, model), F32)
    pad_ref[:, :tc, :] = tokens_ref[...].astype(F32)
    tokens = flat(pad_ref).astype(BF16)
    for cut in blocks:
        x_pre = dot(tokens, w_in_ref[:, cut])
        put(x_pre_ref, cut, x_pre)
        put(x_ref, cut, (x_pre * sigmoid(x_pre)).astype(BF16).astype(F32))
    x_dbl = dot(flat(x_ref).astype(BF16), w_xproj_ref[...])
    xd_ref[:, : rank + 2 * states] = x_dbl
    dt_low = x_dbl[:, :rank].astype(BF16)
    for cut in blocks:
        dt_pre = dot(dt_low, w_dt_ref[:, cut]) + bias_ref[:, cut]
        step = jnp.maximum(dt_pre, 0.0) + jnp.log1p(jnp.exp(-jnp.abs(dt_pre)))
        put(dt_ref, cut, dt_pre)
        put(step_ref, cut, step)
        put(u_ref, cut, step * get(x_ref, cut))
    pad_ref[:, :tc, :] = grad_ref[...].astype(F32)
    grads = flat(pad_ref).astype(BF16)
    for cut in blocks:
        z_pre = dot(tokens, w_in_ref[:, width + cut.start : width + cut.stop])
        gated = dot_transposed(grads, w_out_ref[cut, :])
        put(z_pre_ref, cut, z_pre)
        put(gated_ref, cut, gated)
        put(g_ref, cut, gated * (z_pre * sigmoid(z_pre)))
    for n in range(states):
        spot = pl.ds(n, cells, stride=states)
        for ref, first in ((b_ref, rank), (c_ref, rank + states)):
            column = xd_ref[:, first + n : first + n + 1]
            ref[spot, :] = jnp.broadcast_to(column, (cells, LANES))

    def cell(i, j):
        return pl.ds(pl.multiple_of((i * pad + j) * states, states), states)

    zero = jnp.zeros((states, LANES), F32)

    @pl.loop(0, chunks)
    def _(k):
        cut = lanes(k)
        rate = rates(cut)
        csum = jnp.zeros((pad, LANES), F32)
        for i in range(tr):
            steps = step_ref[i, :, cut]
            csum = csum + steps
            prow[k, i] = jnp.exp2(rate * jnp.sum(steps[:tc], axis=0, keepdims=True))
        for j in range(tc):
            pcol[k, j] = jnp.exp2(rate * csum[j : j + 1])

        def line(count, terms):
            i = tr - 1 - count
            state = zero
            after = []
            for j in range(tc):
                t = i * tc + j
                d = jnp.exp2(rate * step_ref[i, j : j + 1, cut])
                decay[k, t] = d
                state = d * state + u_ref[i, j : j + 1, cut] * b_ref[cell(i, j)]
                after.append(d * (terms[j] + g_ref[i, j : j + 1, cut] * c_ref[cell(i, j)]))
            e1r[k, i] = state
            return tuple(after)

        terms = lax.fori_loop(0, tr, line, (zero,) * tc)
        for j in range(tc):
            e1c[k, j] = terms[j]
        head_send(0, k)
        head_send(1, k)

    @pl.loop(0, chunks)
    def _(k):
        cut = lanes(k)
        forward(0, k)
        forward(1, k)

        def down_line(i, states_in):
            state = in1r[k, i]
            after = []
            for j in range(tc):
                t = i * tc + j
                d = decay[k, t]
                state = d * state + u_ref[i, j : j + 1, cut] * b_ref[cell(i, j)]
                rows[k, t] = state
                after.append(d * states_in[j] + state)
            return tuple(after)

        ends = lax.fori_loop(0, tr, down_line, (zero,) * tc)
        for j in range(tc):
            e2c[k, j] = ends[j]
        head_send(2, k)

        def up_line(count, terms):
            i = tr - 1 - count
            term = zero
            after = [None] * tc
            for j in reversed(range(tc)):
                t = i * tc + j
                d = decay[k, t]
                adjoint = terms[j] + g_ref[i, j : j + 1, cut] * c_ref[cell(i, j)]
                cols[k, t] = adjoint
                after[j] = d * adjoint
                term = d * (adjoint + term)
            e2r[k, i] = term
            return tuple(after)

        lax.fori_loop(0, tr, up_line, tuple(in1c[k, j] for j in range(tc)))
        head_send(3, k)

    bacc_ref[...] = jnp.zeros_like(bacc_ref)
    cacc_ref[...] = jnp.zeros_like(cacc_ref)

    @pl.loop(0, chunks)
    def _(k):
        cut = lanes(k)
        rate = rates(cut)
        forward(2, k)
        forward(3, k)
        for j in range(tc):
            fcar[j] = in2c[k, j]

        def last_line(i, carry):
            term = in2r[k, i]
            for j in reversed(range(tc)):
                t = i * tc + j
                d = decay[k, t]
                adjoint = cols[k, t]
                state = rows[k, t]
                before = in1r[k, i] if j == 0 else rows[k, t - 1]
                passed = d * fcar[j]
                full = passed + state
                fcar[j] = full
                total = adjoint + term
                term = d * total
                slope = adjoint * passed + term * before
                sd_ref[i, j : j + 1, cut] = jnp.sum(slope * rate, axis=0, keepdims=True)
                rb_ref[i, j : j + 1, cut] = jnp.sum(total * b_ref[cell(i, j)], axis=0, keepdims=True)
                out_ref[i, j : j + 1, cut] = jnp.sum(full * c_ref[cell(i, j)], axis=0, keepdims=True)
                bacc_ref[cell(i, j)] += total * u_ref[i, j : j + 1, cut]
                cacc_ref[cell(i, j)] += full * g_ref[i, j : j + 1, cut]
            return carry

        lax.fori_loop(0, tr, last_line, 0)

    both = jnp.zeros((cells, 2 * states), F32)
    lane = lax.broadcasted_iota(jnp.int32, (LANES, 2 * states), 1)
    for n in range(states):
        spot = pl.ds(n, cells, stride=states)
        for ref, at in ((bacc_ref, n), (cacc_ref, states + n)):
            pick = jnp.where(lane == at, 1.0, 0.0).astype(BF16)
            both = both + dot(ref[spot, :].astype(BF16), pick)
    low_grad = jnp.zeros((cells, rank), F32)
    layer = jnp.zeros((cells, model), F32)
    for cut in blocks:
        x, z_pre, dt_pre = get(x_ref, cut), get(z_pre_ref, cut), get(dt_ref, cut)
        scan_out = get(out_ref, cut) + skip_ref[:, cut] * x
        layer = layer + dot((scan_out * (z_pre * sigmoid(z_pre))).astype(BF16), w_out_ref[cut, :])
        put(proj_ref, slice(width + cut.start, width + cut.stop),
            get(gated_ref, cut) * scan_out * silu_grad(z_pre))
        step_grad = get(sd_ref, cut) * math.log(2.0) + get(rb_ref, cut) * x
        low_grad = low_grad + dot_transposed(
            (step_grad * sigmoid(dt_pre)).astype(BF16), w_dt_ref[:, cut]
        )
    layer_ref[...] = layer.reshape(tr, pad, model)[:, :tc, :].astype(BF16)
    xd_ref[:, :rank] = low_grad
    xd_ref[:, rank : rank + 2 * states] = both
    dbl_grad = xd_ref[:, : rank + 2 * states].astype(BF16)
    for cut in blocks:
        x_grad = (
            get(rb_ref, cut) * get(step_ref, cut) + get(g_ref, cut) * skip_ref[:, cut]
            + dot_transposed(dbl_grad, w_xproj_ref[cut, :])
        )
        put(proj_ref, cut, x_grad * silu_grad(get(x_pre_ref, cut)))
    proj = flat(proj_ref).astype(BF16)
    for at in range(0, model, BLOCK):
        token_grad = dot_transposed(proj, w_in_ref[at : at + BLOCK, :])
        token_grad_ref[:, :, at : at + BLOCK] = (
            token_grad.reshape(tr, pad, BLOCK)[:, :tc, :].astype(BF16)
        )

    for kind in range(4):
        tail = links[kind][4]

        @pl.when(jnp.logical_not(tail))
        def _():
            @pl.loop(0, chunks)
            def _(k):
                copy(kind, k).wait_send()


def body(mesh_shape, tokens, w_in, w_xproj, w_dt, dt_bias, a_log, d_skip, w_out, out_grad):
    tr, tc, model = tokens.shape
    rank, width = w_dt.shape
    states = a_log.shape[0]
    chunks = width // LANES
    pad = -(-tc // 16) * 16
    sizes = (mesh_shape["row"], mesh_shape["col"], tr, tc, chunks, states, rank)
    grid_buf = pltpu.VMEM((chunks, tr * tc, states, LANES), F32)
    row_buf = pltpu.VMEM((chunks, tr, states, LANES), F32)
    col_buf = pltpu.VMEM((chunks, tc, states, LANES), F32)
    wide = pltpu.VMEM((tr, pad, width), F32)
    acc = pltpu.VMEM((tr * pad * states, LANES), F32)
    out = jax.ShapeDtypeStruct((tr, tc, model), BF16)
    return pl.pallas_call(
        functools.partial(layer_kernel, sizes),
        out_shape=(out, out),
        in_specs=[pl.BlockSpec(memory_space=pltpu.VMEM)] * 9,
        out_specs=(pl.BlockSpec(memory_space=pltpu.VMEM),) * 2,
        scratch_shapes=[
            pltpu.VMEM((tr, pad, model), F32)] + [wide] * 11 + [
            pltpu.VMEM((tr, pad, 2 * width), F32), pltpu.VMEM((tr * pad, LANES), F32),
            acc, acc, acc, acc,
            grid_buf, grid_buf, grid_buf, row_buf, col_buf,
            row_buf, col_buf, row_buf, col_buf, row_buf, col_buf, row_buf, col_buf,
            pltpu.VMEM((tc, states, LANES), F32),
            pltpu.SemaphoreType.DMA((4, chunks)),
            pltpu.SemaphoreType.DMA((4, chunks)),
        ],
        compiler_params=pltpu.CompilerParams(
            collective_id=0, has_side_effects=True, vmem_limit_bytes=60 * 1024 * 1024
        ),
    )(
        tokens, w_in, w_xproj, w_dt, dt_bias.reshape(1, width), a_log,
        d_skip.reshape(1, width), w_out, out_grad,
    )


def solution(mesh):
    return jax.shard_map(
        functools.partial(body, dict(mesh.shape)),
        mesh=mesh,
        in_specs=(P("row", "col", None), P(), P(), P(), P(), P(), P(), P(), P("row", "col", None)),
        out_specs=(P("row", "col", None), P("row", "col", None)),
        check_vma=False,
    )
```

time: 105 us -> 85.1 us (0.81)
  other arithmetic: 9.06 us -> 0 us
  matrix products: 7.69 us -> 0 us
  local copies, waits for them, and re-layouts: 14.4 us -> 7.65 us
  Pallas kernels: 72.2 us -> 76.5 us
    dot_general x8 -> x0, matrix products: 7.69 us -> none  [the longest x4 4.49 us: dot_transposed(): lax.dot_general(left, right, (((1,), (1,)), ((), ())), preferred_element_...]
    reshape x9 -> x2, local copies, waits for them, and re-layouts: 9.18 us -> 2.55 us  [the longest x1 1.28 us: body(): d_skip.reshape(1, width)]
    pallas_call x1, Pallas kernels: 72.2 us -> 76.5 us  [body(): pl.pallas_call(functools.partial(layer_kernel, sizes), out_shape=(out, ou...]
    reduce_sum x3 -> x0, other arithmetic: 4.19 us -> none  [the longest x1 1.73 us: body(): jnp.sum(bacc, axis=2)]
    unnamed x40 -> x3, local copies, waits for them, and re-layouts: 1.5 us -> 5.1 us
    broadcast_in_dim x2 -> x0, local copies, waits for them, and re-layouts: 2.8 us -> none  [the longest x1 1.41 us: body(): jnp.broadcast_to(b_sel[:, :, None], shape)]
    mul x2 -> x0, other arithmetic: 2.7 us -> none  [the longest x1 1.58 us: body(): -jnp.exp(a_log) * math.log2(math.e)]
    another operation x1 -> x0, other arithmetic: 2.17 us -> none
where the time goes in v1:
time: 85.1 us; the launch traced here: 84.8 us
  Pallas kernels  76.5 us (90%)
  local copies, waits for them, and re-layouts  7.65 us (9%)
    pallas_call x1, Pallas kernels, body(): pl.pallas_call(functools.partial(layer_kernel, sizes), out_shape=(out, ou...  76.5 us
    unnamed x3, local copies, waits for them, and re-layouts  5.1 us

profile of v1, /device:TPU:6, one launch (start us, length us, event | category | flops | bytes accessed | tf_op | source)
XLA Modules:
  0.0 84.8 jit_solution(9222819446634896023)
XLA Ops:
  0.6 1.3 %reshape.10.bias_ref = f32[1,768]{1,0:T(1,128)} reshape(f32[768]{0:T(1024)} %param.13) | data formatting | bytes 6144 | tf_op jit(solution)/shard_map/reshape | solution.py:343
  1.9 1.3 %reshape.11.skip_ref = f32[1,768]{1,0:T(1,128)} reshape(f32[768]{0:T(1024)} %param.15) | data formatting | bytes 6144 | tf_op jit(solution)/shard_map/reshape | solution.py:344
  3.2 1.7 %copy.11.w_xproj_ref = bf16[768,80]{1,0:T(8,128)(2,1)} copy(bf16[768,80]{0,1:T(8,128)(2,1)} %param.11) | data formatting | bytes 245760 | tf_op args[2]
  4.9 76.5 %shard_map.104 = (bf16[12,12,768]{2,1,0:T(8,128)(2,1)}, bf16[12,12,768]{2,1,0:T(8,128)(2,1)}) custom-call(bf16[12,12,768]{2,1,0:T(8,128)(2,1)} %tokens_ref.1, bf16[768,1536]{1,0:T(8,128)(2,1)} %w_in_ref.1, bf16[768,80]{1,0:T(8,128)(2,1)} %copy.11.w_xproj_ref, bf16[48,768]{1,0:T(8,128)(2,1)} %w_dt_ref.1, f32[1,768]{1,0:T(1,128)} %reshape.10.bias_ref, ...), custom_call_target="tpu_custom_call" | custom-call | tf_op jit(solution)/shard_map/pallas_call | solution.py:324
  81.4 1.7 %copy.14 = bf16[12,12,768]{2,1,0:T(8,128)(2,1)} copy(bf16[12,12,768]{2,1,0:T(8,128)(2,1)} %get-tuple-element.4) | data formatting | bytes 442368
  83.1 1.7 %copy.15 = bf16[12,12,768]{2,1,0:T(8,128)(2,1)} copy(bf16[12,12,768]{2,1,0:T(8,128)(2,1)} %get-tuple-element.5) | data formatting | bytes 442368

commit v2 on v1

--- a/solution.py
+++ b/solution.py
@@ -11,6 +11,7 @@
 MESH = pl.DeviceIdType.MESH
 LANES = 128
 BLOCK = 256
+START, LOCAL, COL_HOP, ROW_HOP, SPACE, NEVER = 1000, 1500, 1500, 3000, 2000, 1 << 30
 F32 = jnp.float32
 BF16 = jnp.bfloat16
 
@@ -60,8 +61,6 @@
         @pl.when(jnp.logical_not(edge))
         def _():
             pl.semaphore_signal(barrier, inc=1, device_id=neighbour, device_id_type=MESH)
-    peers = sum(jnp.where(edge, 0, 1) for edge, _ in edges)
-    pl.semaphore_wait(barrier, peers)
 
     links = (
         (e1r, in1r, right, first_col, last_col, prow),
@@ -129,11 +128,11 @@
         x_pre = dot(tokens, w_in_ref[:, cut])
         put(x_pre_ref, cut, x_pre)
         put(x_ref, cut, (x_pre * sigmoid(x_pre)).astype(BF16).astype(F32))
-    x_dbl = dot(flat(x_ref).astype(BF16), w_xproj_ref[...])
+    x_dbl = dot_transposed(flat(x_ref).astype(BF16), w_xproj_ref[...])
     xd_ref[:, : rank + 2 * states] = x_dbl
     dt_low = x_dbl[:, :rank].astype(BF16)
     for cut in blocks:
-        dt_pre = dot(dt_low, w_dt_ref[:, cut]) + bias_ref[:, cut]
+        dt_pre = dot(dt_low, w_dt_ref[:, cut]) + bias_ref[cut].reshape(1, BLOCK)
         step = jnp.maximum(dt_pre, 0.0) + jnp.log1p(jnp.exp(-jnp.abs(dt_pre)))
         put(dt_ref, cut, dt_pre)
         put(step_ref, cut, step)
@@ -157,8 +156,10 @@
 
     zero = jnp.zeros((states, LANES), F32)
 
-    @pl.loop(0, chunks)
-    def _(k):
+    bacc_ref[...] = jnp.zeros_like(bacc_ref)
+    cacc_ref[...] = jnp.zeros_like(cacc_ref)
+
+    def local_ends(k):
         cut = lanes(k)
         rate = rates(cut)
         csum = jnp.zeros((pad, LANES), F32)
@@ -188,11 +189,9 @@
         head_send(0, k)
         head_send(1, k)
 
-    @pl.loop(0, chunks)
-    def _(k):
+    def row_step(k):
         cut = lanes(k)
         forward(0, k)
-        forward(1, k)
 
         def down_line(i, states_in):
             state = in1r[k, i]
@@ -209,6 +208,10 @@
         for j in range(tc):
             e2c[k, j] = ends[j]
         head_send(2, k)
+
+    def col_step(k):
+        cut = lanes(k)
+        forward(1, k)
 
         def up_line(count, terms):
             i = tr - 1 - count
@@ -227,15 +230,15 @@
         lax.fori_loop(0, tr, up_line, tuple(in1c[k, j] for j in range(tc)))
         head_send(3, k)
 
-    bacc_ref[...] = jnp.zeros_like(bacc_ref)
-    cacc_ref[...] = jnp.zeros_like(cacc_ref)
-
-    @pl.loop(0, chunks)
-    def _(k):
+    def col_link(k):
+        forward(2, k)
+
+    def row_link(k):
+        forward(3, k)
+
+    def finish(k):
         cut = lanes(k)
         rate = rates(cut)
-        forward(2, k)
-        forward(3, k)
         for j in range(tc):
             fcar[j] = in2c[k, j]
 
@@ -262,6 +265,40 @@
 
         lax.fori_loop(0, tr, last_line, 0)
 
+    below, after = n_row - 1 - r, n_col - 1 - p
+
+    def col_time(k):
+        return START + LOCAL + COL_HOP * p + ROW_HOP * r + SPACE * k
+
+    def row_time(k):
+        return START + LOCAL + ROW_HOP * below + COL_HOP * after + SPACE * k
+
+    table = (
+        (local_ends, lambda k: START * k),
+        (row_step, lambda k: START + 1 + COL_HOP * p + START * k),
+        (col_step, lambda k: START + 1 + ROW_HOP * below + SPACE * k),
+        (col_link, col_time),
+        (row_link, row_time),
+        (finish, lambda k: jnp.maximum(col_time(k), row_time(k)) + 1),
+    )
+
+    def slot(_, counts):
+        times = [
+            jnp.where(k < chunks, time(k), NEVER) for k, (_, time) in zip(counts, table)
+        ]
+        best = functools.reduce(jnp.minimum, times)
+        free, after_counts = jnp.int32(1), []
+        for k, due, (step, _) in zip(counts, times, table):
+            hit = jnp.where(due == best, free, 0)
+            free = free - hit
+            pl.when(hit == 1)(functools.partial(step, k))
+            after_counts.append(k + hit)
+        return tuple(after_counts)
+
+    peers = sum(jnp.where(edge, 0, 1) for edge, _ in edges)
+    pl.semaphore_wait(barrier, peers)
+    lax.fori_loop(0, len(table) * chunks, slot, (jnp.int32(0),) * len(table))
+
     both = jnp.zeros((cells, 2 * states), F32)
     lane = lax.broadcasted_iota(jnp.int32, (LANES, 2 * states), 1)
     for n in range(states):
@@ -273,7 +310,7 @@
     layer = jnp.zeros((cells, model), F32)
     for cut in blocks:
         x, z_pre, dt_pre = get(x_ref, cut), get(z_pre_ref, cut), get(dt_ref, cut)
-        scan_out = get(out_ref, cut) + skip_ref[:, cut] * x
+        scan_out = get(out_ref, cut) + skip_ref[cut].reshape(1, BLOCK) * x
         layer = layer + dot((scan_out * (z_pre * sigmoid(z_pre))).astype(BF16), w_out_ref[cut, :])
         put(proj_ref, slice(width + cut.start, width + cut.stop),
             get(gated_ref, cut) * scan_out * silu_grad(z_pre))
@@ -287,8 +324,8 @@
     dbl_grad = xd_ref[:, : rank + 2 * states].astype(BF16)
     for cut in blocks:
         x_grad = (
-            get(rb_ref, cut) * get(step_ref, cut) + get(g_ref, cut) * skip_ref[:, cut]
-            + dot_transposed(dbl_grad, w_xproj_ref[cut, :])
+            get(rb_ref, cut) * get(step_ref, cut) + get(g_ref, cut) * skip_ref[cut].reshape(1, BLOCK)
+            + dot(dbl_grad, w_xproj_ref[:, cut])
         )
         put(proj_ref, cut, x_grad * silu_grad(get(x_pre_ref, cut)))
     proj = flat(proj_ref).astype(BF16)
@@ -340,8 +377,7 @@
             collective_id=0, has_side_effects=True, vmem_limit_bytes=60 * 1024 * 1024
         ),
     )(
-        tokens, w_in, w_xproj, w_dt, dt_bias.reshape(1, width), a_log,
-        d_skip.reshape(1, width), w_out, out_grad,
+        tokens, w_in, w_xproj.T, w_dt, dt_bias, a_log, d_skip, w_out, out_grad,
     )
 
 

time: 85.1 us -> 65.9 us (0.77)
  the two profiles are of different devices: /device:TPU:6 before, /device:TPU:0 now
where the time goes in v2:
time: 65.9 us; the launch traced here: 65.8 us
  Pallas kernels  61.7 us (94%)
  local copies, waits for them, and re-layouts  3.39 us (5%)
    pallas_call x1, Pallas kernels, body(): pl.pallas_call(functools.partial(layer_kernel, sizes), out_shape=(out, ou...  61.7 us
    unnamed x2, local copies, waits for them, and re-layouts  3.39 us

profile of v2, /device:TPU:0, one launch (start us, length us, event | category | flops | bytes accessed | tf_op | source)
XLA Modules:
  0.0 65.8 jit_solution(17201318734396877120)
XLA Ops:
  0.6 61.7 %shard_map.104 = (bf16[12,12,768]{2,1,0:T(8,128)(2,1)}, bf16[12,12,768]{2,1,0:T(8,128)(2,1)}) custom-call(bf16[12,12,768]{2,1,0:T(8,128)(2,1)} %tokens_ref.1, bf16[768,1536]{1,0:T(8,128)(2,1)} %w_in_ref.1, bf16[80,768]{1,0:T(8,128)(2,1)} %bitcast.1, bf16[48,768]{1,0:T(8,128)(2,1)} %w_dt_ref.1, f32[768]{0:T(1024)} %bias_ref.1, f32[16,768]{1,0:T(8,128)} %a_log_ref.1, ...), custom_call_target="tpu_custom_call" | custom-call | tf_op jit(solution)/shard_map/pallas_call | solution.py:361
  62.4 1.7 %copy.13 = bf16[12,12,768]{2,1,0:T(8,128)(2,1)} copy(bf16[12,12,768]{2,1,0:T(8,128)(2,1)} %get-tuple-element.4) | data formatting | bytes 442368
  64.1 1.7 %copy.14 = bf16[12,12,768]{2,1,0:T(8,128)(2,1)} copy(bf16[12,12,768]{2,1,0:T(8,128)(2,1)} %get-tuple-element.5) | data formatting | bytes 442368

commit v3 on v2

--- a/solution.py
+++ b/solution.py
@@ -38,7 +38,7 @@
     tokens_ref, w_in_ref, w_xproj_ref, w_dt_ref, bias_ref, a_log_ref, skip_ref, w_out_ref, grad_ref,
     layer_ref, token_grad_ref,
     pad_ref, x_pre_ref, z_pre_ref, x_ref, step_ref, u_ref, g_ref, gated_ref, dt_ref,
-    out_ref, rb_ref, sd_ref, proj_ref, xd_ref, b_ref, c_ref, bacc_ref, cacc_ref,
+    out_ref, rb_ref, sd_ref, proj_ref, xd_ref, b_ref, c_ref, bacc_ref, cacc_ref, b_diag, c_diag,
     decay, rows, cols, prow, pcol,
     e1r, e1c, e2r, e2c, in1r, in1c, in2r, in2c, fcar,
     send_sem, recv_sem,
@@ -151,6 +151,18 @@
             column = xd_ref[:, first + n : first + n + 1]
             ref[spot, :] = jnp.broadcast_to(column, (cells, LANES))
 
+    place = lax.broadcasted_iota(jnp.int32, (tr, pad, tc * states), 1)
+    group = lax.broadcasted_iota(jnp.int32, (tr, pad, tc * states), 2) // states
+    on_diag = place == group
+    repeat = jnp.where(
+        lax.broadcasted_iota(jnp.int32, (states, tc * states), 1) % states
+        == lax.broadcasted_iota(jnp.int32, (states, tc * states), 0), 1.0, 0.0
+    ).astype(BF16)
+    for ref, first in ((b_diag, rank), (c_diag, rank + states)):
+        spread = dot(x_dbl[:, first : first + states].astype(BF16), repeat)
+        ref[...] = jnp.where(on_diag, spread.reshape(tr, pad, tc * states), 0.0).astype(BF16)
+    ones_diag = jnp.where(on_diag[0], 1.0, 0.0).astype(BF16)
+
     def cell(i, j):
         return pl.ds(pl.multiple_of((i * pad + j) * states, states), states)
 
@@ -244,23 +256,31 @@
 
         def last_line(i, carry):
             term = in2r[k, i]
+            state = rows[k, i * tc + tc - 1]
+            fulls, totals, slopes = [], [], []
             for j in reversed(range(tc)):
                 t = i * tc + j
                 d = decay[k, t]
                 adjoint = cols[k, t]
-                state = rows[k, t]
                 before = in1r[k, i] if j == 0 else rows[k, t - 1]
                 passed = d * fcar[j]
                 full = passed + state
                 fcar[j] = full
                 total = adjoint + term
                 term = d * total
-                slope = adjoint * passed + term * before
-                sd_ref[i, j : j + 1, cut] = jnp.sum(slope * rate, axis=0, keepdims=True)
-                rb_ref[i, j : j + 1, cut] = jnp.sum(total * b_ref[cell(i, j)], axis=0, keepdims=True)
-                out_ref[i, j : j + 1, cut] = jnp.sum(full * c_ref[cell(i, j)], axis=0, keepdims=True)
-                bacc_ref[cell(i, j)] += total * u_ref[i, j : j + 1, cut]
-                cacc_ref[cell(i, j)] += full * g_ref[i, j : j + 1, cut]
+                slope = (adjoint * passed + term * before) * rate
+                state = before
+                fulls.insert(0, full.astype(BF16))
+                totals.insert(0, total.astype(BF16))
+                slopes.insert(0, slope.astype(BF16))
+            fulls, totals, slopes = (
+                jnp.concatenate(parts, axis=0) for parts in (fulls, totals, slopes)
+            )
+            out_ref[i, :, cut] = dot(c_diag[i], fulls)
+            rb_ref[i, :, cut] = dot(b_diag[i], totals)
+            sd_ref[i, :, cut] = dot(ones_diag, slopes)
+            bacc_ref[i] += dot_transposed(u_ref[i, :, cut].astype(BF16), totals)
+            cacc_ref[i] += dot_transposed(g_ref[i, :, cut].astype(BF16), fulls)
             return carry
 
         lax.fori_loop(0, tr, last_line, 0)
@@ -300,12 +320,12 @@
     lax.fori_loop(0, len(table) * chunks, slot, (jnp.int32(0),) * len(table))
 
     both = jnp.zeros((cells, 2 * states), F32)
-    lane = lax.broadcasted_iota(jnp.int32, (LANES, 2 * states), 1)
-    for n in range(states):
-        spot = pl.ds(n, cells, stride=states)
-        for ref, at in ((bacc_ref, n), (cacc_ref, states + n)):
-            pick = jnp.where(lane == at, 1.0, 0.0).astype(BF16)
-            both = both + dot(ref[spot, :].astype(BF16), pick)
+    spot = lax.broadcasted_iota(jnp.int32, (tc * states, 2 * states), 0) % states
+    lane = lax.broadcasted_iota(jnp.int32, (tc * states, 2 * states), 1)
+    for ref, first in ((bacc_ref, 0), (cacc_ref, states)):
+        pick = jnp.where(lane == spot + first, 1.0, 0.0).astype(BF16)
+        kept = jnp.where(on_diag, ref[...], 0.0).reshape(cells, tc * states)
+        both = both + dot(kept.astype(BF16), pick)
     low_grad = jnp.zeros((cells, rank), F32)
     layer = jnp.zeros((cells, model), F32)
     for cut in blocks:
@@ -357,6 +377,7 @@
     col_buf = pltpu.VMEM((chunks, tc, states, LANES), F32)
     wide = pltpu.VMEM((tr, pad, width), F32)
     acc = pltpu.VMEM((tr * pad * states, LANES), F32)
+    diag = functools.partial(pltpu.VMEM, (tr, pad, tc * states))
     out = jax.ShapeDtypeStruct((tr, tc, model), BF16)
     return pl.pallas_call(
         functools.partial(layer_kernel, sizes),
@@ -366,7 +387,7 @@
         scratch_shapes=[
             pltpu.VMEM((tr, pad, model), F32)] + [wide] * 11 + [
             pltpu.VMEM((tr, pad, 2 * width), F32), pltpu.VMEM((tr * pad, LANES), F32),
-            acc, acc, acc, acc,
+            acc, acc, diag(F32), diag(F32), diag(BF16), diag(BF16),
             grid_buf, grid_buf, grid_buf, row_buf, col_buf,
             row_buf, col_buf, row_buf, col_buf, row_buf, col_buf, row_buf, col_buf,
             pltpu.VMEM((tc, states, LANES), F32),

time: 65.9 us -> 69.4 us (1.053)
  Pallas kernels: 61.7 us -> 65.2 us
    pallas_call x1, Pallas kernels: 61.7 us -> 65.2 us  [body(): pl.pallas_call(functools.partial(layer_kernel, sizes), out_shape=(out, ou...]
where the time goes in v3:
time: 69.4 us; the launch traced here: 69.2 us
  Pallas kernels  65.2 us (94%)
  local copies, waits for them, and re-layouts  3.39 us (5%)
    pallas_call x1, Pallas kernels, body(): pl.pallas_call(functools.partial(layer_kernel, sizes), out_shape=(out, ou...  65.2 us
    unnamed x2, local copies, waits for them, and re-layouts  3.39 us

profile of v3, /device:TPU:0, one launch (start us, length us, event | category | flops | bytes accessed | tf_op | source)
XLA Modules:
  0.0 69.2 jit_solution(13814817559295897321)
XLA Ops:
  0.6 65.2 %shard_map.104 = (bf16[12,12,768]{2,1,0:T(8,128)(2,1)}, bf16[12,12,768]{2,1,0:T(8,128)(2,1)}) custom-call(bf16[12,12,768]{2,1,0:T(8,128)(2,1)} %tokens_ref.1, bf16[768,1536]{1,0:T(8,128)(2,1)} %w_in_ref.1, bf16[80,768]{1,0:T(8,128)(2,1)} %bitcast.1, bf16[48,768]{1,0:T(8,128)(2,1)} %w_dt_ref.1, f32[768]{0:T(1024)} %bias_ref.1, f32[16,768]{1,0:T(8,128)} %a_log_ref.1, ...), custom_call_target="tpu_custom_call" | custom-call | tf_op jit(solution)/shard_map/pallas_call | solution.py:382
  65.8 1.7 %copy.13 = bf16[12,12,768]{2,1,0:T(8,128)(2,1)} copy(bf16[12,12,768]{2,1,0:T(8,128)(2,1)} %get-tuple-element.4) | data formatting | bytes 442368
  67.5 1.7 %copy.14 = bf16[12,12,768]{2,1,0:T(8,128)(2,1)} copy(bf16[12,12,768]{2,1,0:T(8,128)(2,1)} %get-tuple-element.5) | data formatting | bytes 442368

commit v4 on v2

--- a/solution.py
+++ b/solution.py
@@ -11,7 +11,7 @@
 MESH = pl.DeviceIdType.MESH
 LANES = 128
 BLOCK = 256
-START, LOCAL, COL_HOP, ROW_HOP, SPACE, NEVER = 1000, 1500, 1500, 3000, 2000, 1 << 30
+START, LOCAL, COL_HOP, ROW_HOP, SPACE, NEVER = 1000, 1500, 2500, 3000, 2000, 1 << 30
 F32 = jnp.float32
 BF16 = jnp.bfloat16
 
@@ -39,9 +39,10 @@
     layer_ref, token_grad_ref,
     pad_ref, x_pre_ref, z_pre_ref, x_ref, step_ref, u_ref, g_ref, gated_ref, dt_ref,
     out_ref, rb_ref, sd_ref, proj_ref, xd_ref, b_ref, c_ref, bacc_ref, cacc_ref,
-    decay, rows, cols, prow, pcol,
-    e1r, e1c, e2r, e2c, in1r, in1c, in2r, in2c, fcar,
-    send_sem, recv_sem,
+    decay, rows, cols, prow, pcol, mate_prow, mate_pcol,
+    e1r, e1c, e2r, e2c, in1r, in1c, in2r, in2c, s1r, s1c, s2r, s2c, o1r, o1c, o2r, o2c, fcar,
+    rsum, csum, mate_rsum, mate_csum,
+    send_sem, recv_sem, swap_send, swap_recv, sum_send, sum_recv,
 ):
     n_row, n_col, tr, tc, chunks, states, rank = sizes
     pad = pad_ref.shape[1]
@@ -50,65 +51,110 @@
     model = pad_ref.shape[-1]
     r = lax.axis_index("row")
     p = lax.axis_index("col")
-    left, right = (r, lax.rem(p + n_col - 1, n_col)), (r, lax.rem(p + 1, n_col))
-    up, down = (lax.rem(r + n_row - 1, n_row), p), (lax.rem(r + 1, n_row), p)
-    first_col, last_col = p == 0, p == n_col - 1
-    first_row, last_row = r == 0, r == n_row - 1
+    col_mate, row_mate = (r, p + 1 - 2 * (p % 2)), (r + 1 - 2 * (r % 2), p)
+    right, left = (r, (p + 2) % n_col), (r, (p + n_col - 2) % n_col)
+    down, up = ((r + 2) % n_row, p), ((r + n_row - 2) % n_row, p)
+    first_col, last_col = p // 2 == 0, p // 2 == n_col // 2 - 1
+    first_row, last_row = r // 2 == 0, r // 2 == n_row // 2 - 1
 
     barrier = pltpu.get_barrier_semaphore()
     edges = ((first_col, left), (last_col, right), (first_row, up), (last_row, down))
+    for mate in (col_mate, row_mate):
+        pl.semaphore_signal(barrier, inc=1, device_id=mate, device_id_type=MESH)
     for edge, neighbour in edges:
         @pl.when(jnp.logical_not(edge))
         def _():
             pl.semaphore_signal(barrier, inc=1, device_id=neighbour, device_id_type=MESH)
 
     links = (
-        (e1r, in1r, right, first_col, last_col, prow),
-        (e1c, in1c, up, last_row, first_row, pcol),
-        (e2c, in2c, down, first_row, last_row, pcol),
-        (e2r, in2r, left, last_col, first_col, prow),
+        (e1r, in1r, s1r, o1r, prow, mate_prow, col_mate, right, first_col, last_col, p % 2 == 1),
+        (e1c, in1c, s1c, o1c, pcol, mate_pcol, row_mate, up, last_row, first_row, r % 2 == 0),
+        (e2c, in2c, s2c, o2c, pcol, mate_pcol, row_mate, down, first_row, last_row, r % 2 == 1),
+        (e2r, in2r, s2r, o2r, prow, mate_prow, col_mate, left, last_col, first_col, p % 2 == 0),
     )
 
-    def copy(kind, k):
-        source, target, where = links[kind][:3]
+    def both(one, other):
+        return jnp.logical_and(one, other)
+
+    def swap(kind, k):
         return pltpu.make_async_remote_copy(
-            src_ref=source.at[k],
-            dst_ref=target.at[k],
+            src_ref=links[kind][0].at[k],
+            dst_ref=links[kind][1].at[k],
+            send_sem=swap_send.at[kind, k],
+            recv_sem=swap_recv.at[kind, k],
+            device_id=links[kind][6],
+            device_id_type=MESH,
+        )
+
+    def onward(kind, k):
+        return pltpu.make_async_remote_copy(
+            src_ref=links[kind][3].at[k],
+            dst_ref=links[kind][2].at[k],
             send_sem=send_sem.at[kind, k],
             recv_sem=recv_sem.at[kind, k],
-            device_id=where,
+            device_id=links[kind][7],
             device_id_type=MESH,
         )
 
+    def sum_copy(way):
+        source, target, mate = ((rsum, mate_rsum, col_mate), (csum, mate_csum, row_mate))[way]
+        return pltpu.make_async_remote_copy(
+            src_ref=source,
+            dst_ref=target,
+            send_sem=sum_send.at[way],
+            recv_sem=sum_recv.at[way],
+            device_id=mate,
+            device_id_type=MESH,
+        )
+
     for kind in range(4):
-        @pl.when(links[kind][3])
-        def _():
-            links[kind][1][...] = jnp.zeros_like(links[kind][1])
+        @pl.when(links[kind][8])
+        def _():
+            links[kind][2][...] = jnp.zeros_like(links[kind][2])
 
     def head_send(kind, k):
-        head, tail = links[kind][3:5]
-
-        @pl.when(jnp.logical_and(head, jnp.logical_not(tail)))
-        def _():
-            copy(kind, k).start()
+        last, second = links[kind][9:]
+
+        @pl.when(jnp.logical_not(both(last, second)))
+        def _():
+            swap(kind, k).start()
 
     def forward(kind, k):
-        source, target, _, head, tail, product = links[kind]
-
-        @pl.when(jnp.logical_not(head))
-        def _():
-            copy(kind, k).wait_recv()
-
-        @pl.when(jnp.logical_not(jnp.logical_or(head, tail)))
-        def _():
-            source[k] = source[k] + product[k] * target[k]
-            copy(kind, k).start()
+        own, into, enter, leave, here, there = links[kind][:6]
+        first, last, second = links[kind][8:]
+        prior = jnp.logical_not(second)
+
+        @pl.when(jnp.logical_not(both(last, prior)))
+        def _():
+            swap(kind, k).wait_recv()
+
+        @pl.when(jnp.logical_not(first))
+        def _():
+            onward(kind, k).wait_recv()
+
+        @pl.when(both(jnp.logical_not(last), second))
+        def _():
+            leave[k] = own[k] + here[k] * (into[k] + there[k] * enter[k])
+            onward(kind, k).start()
+
+        @pl.when(both(jnp.logical_not(last), prior))
+        def _():
+            leave[k] = into[k] + there[k] * (own[k] + here[k] * enter[k])
+            onward(kind, k).start()
+
+        @pl.when(second)
+        def _():
+            into[k] = into[k] + there[k] * enter[k]
+
+        @pl.when(prior)
+        def _():
+            into[k] = enter[k]
+
+    def lanes(k):
+        return pl.ds(pl.multiple_of(k * LANES, LANES), LANES)
 
     def rates(cut):
         return jnp.exp(a_log_ref[:, cut]) * -math.log2(math.e)
-
-    def lanes(k):
-        return pl.ds(pl.multiple_of(k * LANES, LANES), LANES)
 
     def flat(ref):
         return ref[...].reshape(cells, ref.shape[-1])
@@ -137,6 +183,17 @@
         put(dt_ref, cut, dt_pre)
         put(step_ref, cut, step)
         put(u_ref, cut, step * get(x_ref, cut))
+    for cut in blocks:
+        totals = jnp.zeros((pad, BLOCK), F32)
+        for i in range(tr):
+            steps = step_ref[i, :, cut]
+            totals = totals + steps
+            rsum[i : i + 1, cut] = jnp.sum(steps[:tc], axis=0, keepdims=True)
+        csum[:, cut] = totals[:tc]
+    peers = 2 + sum(jnp.where(edge, 0, 1) for edge, _ in edges)
+    pl.semaphore_wait(barrier, peers)
+    for way in range(2):
+        sum_copy(way).start()
     pad_ref[:, :tc, :] = grad_ref[...].astype(F32)
     grads = flat(pad_ref).astype(BF16)
     for cut in blocks:
@@ -162,13 +219,12 @@
     def local_ends(k):
         cut = lanes(k)
         rate = rates(cut)
-        csum = jnp.zeros((pad, LANES), F32)
         for i in range(tr):
-            steps = step_ref[i, :, cut]
-            csum = csum + steps
-            prow[k, i] = jnp.exp2(rate * jnp.sum(steps[:tc], axis=0, keepdims=True))
+            prow[k, i] = jnp.exp2(rate * rsum[i : i + 1, cut])
+            mate_prow[k, i] = jnp.exp2(rate * mate_rsum[i : i + 1, cut])
         for j in range(tc):
-            pcol[k, j] = jnp.exp2(rate * csum[j : j + 1])
+            pcol[k, j] = jnp.exp2(rate * csum[j : j + 1, cut])
+            mate_pcol[k, j] = jnp.exp2(rate * mate_csum[j : j + 1, cut])
 
         def line(count, terms):
             i = tr - 1 - count
@@ -265,17 +321,17 @@
 
         lax.fori_loop(0, tr, last_line, 0)
 
-    below, after = n_row - 1 - r, n_col - 1 - p
+    below, after = (n_row - 1 - r) // 2, (n_col - 1 - p) // 2
 
     def col_time(k):
-        return START + LOCAL + COL_HOP * p + ROW_HOP * r + SPACE * k
+        return START + LOCAL + COL_HOP * (p // 2) + ROW_HOP * (r // 2) + SPACE * k
 
     def row_time(k):
         return START + LOCAL + ROW_HOP * below + COL_HOP * after + SPACE * k
 
     table = (
         (local_ends, lambda k: START * k),
-        (row_step, lambda k: START + 1 + COL_HOP * p + START * k),
+        (row_step, lambda k: START + 1 + COL_HOP * (p // 2) + START * k),
         (col_step, lambda k: START + 1 + ROW_HOP * below + SPACE * k),
         (col_link, col_time),
         (row_link, row_time),
@@ -295,17 +351,17 @@
             after_counts.append(k + hit)
         return tuple(after_counts)
 
-    peers = sum(jnp.where(edge, 0, 1) for edge, _ in edges)
-    pl.semaphore_wait(barrier, peers)
+    for way in range(2):
+        sum_copy(way).wait_recv()
     lax.fori_loop(0, len(table) * chunks, slot, (jnp.int32(0),) * len(table))
 
-    both = jnp.zeros((cells, 2 * states), F32)
+    narrow = jnp.zeros((cells, 2 * states), F32)
     lane = lax.broadcasted_iota(jnp.int32, (LANES, 2 * states), 1)
     for n in range(states):
         spot = pl.ds(n, cells, stride=states)
         for ref, at in ((bacc_ref, n), (cacc_ref, states + n)):
             pick = jnp.where(lane == at, 1.0, 0.0).astype(BF16)
-            both = both + dot(ref[spot, :].astype(BF16), pick)
+            narrow = narrow + dot(ref[spot, :].astype(BF16), pick)
     low_grad = jnp.zeros((cells, rank), F32)
     layer = jnp.zeros((cells, model), F32)
     for cut in blocks:
@@ -320,7 +376,7 @@
         )
     layer_ref[...] = layer.reshape(tr, pad, model)[:, :tc, :].astype(BF16)
     xd_ref[:, :rank] = low_grad
-    xd_ref[:, rank : rank + 2 * states] = both
+    xd_ref[:, rank : rank + 2 * states] = narrow
     dbl_grad = xd_ref[:, : rank + 2 * states].astype(BF16)
     for cut in blocks:
         x_grad = (
@@ -335,14 +391,22 @@
             token_grad.reshape(tr, pad, BLOCK)[:, :tc, :].astype(BF16)
         )
 
+    for way in range(2):
+        sum_copy(way).wait_send()
     for kind in range(4):
-        tail = links[kind][4]
-
-        @pl.when(jnp.logical_not(tail))
+        last, second = links[kind][9:]
+
+        @pl.when(jnp.logical_not(last))
         def _():
             @pl.loop(0, chunks)
             def _(k):
-                copy(kind, k).wait_send()
+                onward(kind, k).wait_send()
+
+        @pl.when(jnp.logical_not(both(last, second)))
+        def _():
+            @pl.loop(0, chunks)
+            def _(k):
+                swap(kind, k).wait_send()
 
 
 def body(mesh_shape, tokens, w_in, w_xproj, w_dt, dt_bias, a_log, d_skip, w_out, out_grad):
@@ -367,11 +431,12 @@
             pltpu.VMEM((tr, pad, model), F32)] + [wide] * 11 + [
             pltpu.VMEM((tr, pad, 2 * width), F32), pltpu.VMEM((tr * pad, LANES), F32),
             acc, acc, acc, acc,
-            grid_buf, grid_buf, grid_buf, row_buf, col_buf,
-            row_buf, col_buf, row_buf, col_buf, row_buf, col_buf, row_buf, col_buf,
+            grid_buf, grid_buf, grid_buf, row_buf, col_buf, row_buf, col_buf,
+        ] + [row_buf, col_buf, row_buf, col_buf] * 4 + [
             pltpu.VMEM((tc, states, LANES), F32),
-            pltpu.SemaphoreType.DMA((4, chunks)),
-            pltpu.SemaphoreType.DMA((4, chunks)),
+            pltpu.VMEM((tr, width), F32), pltpu.VMEM((tc, width), F32),
+            pltpu.VMEM((tr, width), F32), pltpu.VMEM((tc, width), F32),
+        ] + [pltpu.SemaphoreType.DMA((4, chunks))] * 4 + [pltpu.SemaphoreType.DMA((2,))] * 2 + [
         ],
         compiler_params=pltpu.CompilerParams(
             collective_id=0, has_side_effects=True, vmem_limit_bytes=60 * 1024 * 1024

time: 65.9 us -> 61.5 us (0.933)
  Pallas kernels: 61.7 us -> 57.3 us
    pallas_call x1, Pallas kernels: 61.7 us -> 57.3 us  [body(): pl.pallas_call(functools.partial(layer_kernel, sizes), out_shape=(out, ou...]
where the time goes in v4:
time: 61.5 us; the launch traced here: 61.3 us
  Pallas kernels  57.3 us (93%)
  local copies, waits for them, and re-layouts  3.39 us (6%)
  between operations  0.64 us (1%)
    pallas_call x1, Pallas kernels, body(): pl.pallas_call(functools.partial(layer_kernel, sizes), out_shape=(out, ou...  57.3 us
    unnamed x2, local copies, waits for them, and re-layouts  3.39 us

profile of v4, /device:TPU:0, one launch (start us, length us, event | category | flops | bytes accessed | tf_op | source)
XLA Modules:
  0.0 61.3 jit_solution(4490567197675717743)
XLA Ops:
  0.6 57.3 %shard_map.104 = (bf16[12,12,768]{2,1,0:T(8,128)(2,1)}, bf16[12,12,768]{2,1,0:T(8,128)(2,1)}) custom-call(bf16[12,12,768]{2,1,0:T(8,128)(2,1)} %tokens_ref.1, bf16[768,1536]{1,0:T(8,128)(2,1)} %w_in_ref.1, bf16[80,768]{1,0:T(8,128)(2,1)} %bitcast.1, bf16[48,768]{1,0:T(8,128)(2,1)} %w_dt_ref.1, f32[768]{0:T(1024)} %bias_ref.1, f32[16,768]{1,0:T(8,128)} %a_log_ref.1, ...), custom_call_target="tpu_custom_call" | custom-call | tf_op jit(solution)/shard_map/pallas_call | solution.py:425
  58.0 1.7 %copy.13 = bf16[12,12,768]{2,1,0:T(8,128)(2,1)} copy(bf16[12,12,768]{2,1,0:T(8,128)(2,1)} %get-tuple-element.4) | data formatting | bytes 442368
  59.7 1.7 %copy.14 = bf16[12,12,768]{2,1,0:T(8,128)(2,1)} copy(bf16[12,12,768]{2,1,0:T(8,128)(2,1)} %get-tuple-element.5) | data formatting | bytes 442368

commit v5 on v4

--- a/solution.py
+++ b/solution.py
@@ -208,8 +208,12 @@
             column = xd_ref[:, first + n : first + n + 1]
             ref[spot, :] = jnp.broadcast_to(column, (cells, LANES))
 
-    def cell(i, j):
-        return pl.ds(pl.multiple_of((i * pad + j) * states, states), states)
+    def tile_row(ref, i):
+        size = pad * states
+        return ref.at[pl.ds(pl.multiple_of(i * size, size), size)]
+
+    def cell(j):
+        return slice(j * states, (j + 1) * states)
 
     zero = jnp.zeros((states, LANES), F32)
 
@@ -228,18 +232,18 @@
 
         def line(count, terms):
             i = tr - 1 - count
+            b_row, c_row = tile_row(b_ref, i), tile_row(c_ref, i)
             state = zero
             after = []
             for j in range(tc):
-                t = i * tc + j
                 d = jnp.exp2(rate * step_ref[i, j : j + 1, cut])
-                decay[k, t] = d
-                state = d * state + u_ref[i, j : j + 1, cut] * b_ref[cell(i, j)]
-                after.append(d * (terms[j] + g_ref[i, j : j + 1, cut] * c_ref[cell(i, j)]))
+                decay[k, i, j] = d
+                state = d * state + u_ref[i, j : j + 1, cut] * b_row[cell(j)]
+                after.append(d * (terms[j] + g_ref[i, j : j + 1, cut] * c_row[cell(j)]))
             e1r[k, i] = state
             return tuple(after)
 
-        terms = lax.fori_loop(0, tr, line, (zero,) * tc)
+        terms = lax.fori_loop(0, tr, line, (zero,) * tc, unroll=2)
         for j in range(tc):
             e1c[k, j] = terms[j]
         head_send(0, k)
@@ -250,17 +254,17 @@
         forward(0, k)
 
         def down_line(i, states_in):
+            b_row = tile_row(b_ref, i)
             state = in1r[k, i]
             after = []
             for j in range(tc):
-                t = i * tc + j
-                d = decay[k, t]
-                state = d * state + u_ref[i, j : j + 1, cut] * b_ref[cell(i, j)]
-                rows[k, t] = state
+                d = decay[k, i, j]
+                state = d * state + u_ref[i, j : j + 1, cut] * b_row[cell(j)]
+                rows[k, i, j] = state
                 after.append(d * states_in[j] + state)
             return tuple(after)
 
-        ends = lax.fori_loop(0, tr, down_line, (zero,) * tc)
+        ends = lax.fori_loop(0, tr, down_line, (zero,) * tc, unroll=2)
         for j in range(tc):
             e2c[k, j] = ends[j]
         head_send(2, k)
@@ -271,19 +275,19 @@
 
         def up_line(count, terms):
             i = tr - 1 - count
+            c_row = tile_row(c_ref, i)
             term = zero
             after = [None] * tc
             for j in reversed(range(tc)):
-                t = i * tc + j
-                d = decay[k, t]
-                adjoint = terms[j] + g_ref[i, j : j + 1, cut] * c_ref[cell(i, j)]
-                cols[k, t] = adjoint
+                d = decay[k, i, j]
+                adjoint = terms[j] + g_ref[i, j : j + 1, cut] * c_row[cell(j)]
+                cols[k, i, j] = adjoint
                 after[j] = d * adjoint
                 term = d * (adjoint + term)
             e2r[k, i] = term
             return tuple(after)
 
-        lax.fori_loop(0, tr, up_line, tuple(in1c[k, j] for j in range(tc)))
+        lax.fori_loop(0, tr, up_line, tuple(in1c[k, j] for j in range(tc)), unroll=2)
         head_send(3, k)
 
     def col_link(k):
@@ -299,27 +303,29 @@
             fcar[j] = in2c[k, j]
 
         def last_line(i, carry):
+            b_row, c_row = tile_row(b_ref, i), tile_row(c_ref, i)
+            bacc_row, cacc_row = tile_row(bacc_ref, i), tile_row(cacc_ref, i)
             term = in2r[k, i]
+            state = rows[k, i, tc - 1]
             for j in reversed(range(tc)):
-                t = i * tc + j
-                d = decay[k, t]
-                adjoint = cols[k, t]
-                state = rows[k, t]
-                before = in1r[k, i] if j == 0 else rows[k, t - 1]
+                d = decay[k, i, j]
+                adjoint = cols[k, i, j]
+                before = in1r[k, i] if j == 0 else rows[k, i, j - 1]
                 passed = d * fcar[j]
                 full = passed + state
                 fcar[j] = full
                 total = adjoint + term
                 term = d * total
                 slope = adjoint * passed + term * before
+                state = before
                 sd_ref[i, j : j + 1, cut] = jnp.sum(slope * rate, axis=0, keepdims=True)
-                rb_ref[i, j : j + 1, cut] = jnp.sum(total * b_ref[cell(i, j)], axis=0, keepdims=True)
-                out_ref[i, j : j + 1, cut] = jnp.sum(full * c_ref[cell(i, j)], axis=0, keepdims=True)
-                bacc_ref[cell(i, j)] += total * u_ref[i, j : j + 1, cut]
-                cacc_ref[cell(i, j)] += full * g_ref[i, j : j + 1, cut]
+                rb_ref[i, j : j + 1, cut] = jnp.sum(total * b_row[cell(j)], axis=0, keepdims=True)
+                out_ref[i, j : j + 1, cut] = jnp.sum(full * c_row[cell(j)], axis=0, keepdims=True)
+                bacc_row[cell(j)] += total * u_ref[i, j : j + 1, cut]
+                cacc_row[cell(j)] += full * g_ref[i, j : j + 1, cut]
             return carry
 
-        lax.fori_loop(0, tr, last_line, 0)
+        lax.fori_loop(0, tr, last_line, 0, unroll=2)
 
     below, after = (n_row - 1 - r) // 2, (n_col - 1 - p) // 2
 
@@ -416,7 +422,7 @@
     chunks = width // LANES
     pad = -(-tc // 16) * 16
     sizes = (mesh_shape["row"], mesh_shape["col"], tr, tc, chunks, states, rank)
-    grid_buf = pltpu.VMEM((chunks, tr * tc, states, LANES), F32)
+    grid_buf = pltpu.VMEM((chunks, tr, tc, states, LANES), F32)
     row_buf = pltpu.VMEM((chunks, tr, states, LANES), F32)
     col_buf = pltpu.VMEM((chunks, tc, states, LANES), F32)
     wide = pltpu.VMEM((tr, pad, width), F32)

time: 61.5 us -> 60.8 us (0.989)
  Pallas kernels: 57.3 us -> 56.6 us
    pallas_call x1, Pallas kernels: 57.3 us -> 56.6 us  [body(): pl.pallas_call(functools.partial(layer_kernel, sizes), out_shape=(out, ou...]
where the time goes in v5:
time: 60.8 us; the launch traced here: 60.6 us
  Pallas kernels  56.6 us (93%)
  local copies, waits for them, and re-layouts  3.39 us (6%)
  between operations  0.64 us (1%)
    pallas_call x1, Pallas kernels, body(): pl.pallas_call(functools.partial(layer_kernel, sizes), out_shape=(out, ou...  56.6 us
    unnamed x2, local copies, waits for them, and re-layouts  3.39 us

profile of v5, /device:TPU:0, one launch (start us, length us, event | category | flops | bytes accessed | tf_op | source)
XLA Modules:
  0.0 60.6 jit_solution(10480010697769619018)
XLA Ops:
  0.6 56.6 %shard_map.104 = (bf16[12,12,768]{2,1,0:T(8,128)(2,1)}, bf16[12,12,768]{2,1,0:T(8,128)(2,1)}) custom-call(bf16[12,12,768]{2,1,0:T(8,128)(2,1)} %tokens_ref.1, bf16[768,1536]{1,0:T(8,128)(2,1)} %w_in_ref.1, bf16[80,768]{1,0:T(8,128)(2,1)} %bitcast.1, bf16[48,768]{1,0:T(8,128)(2,1)} %w_dt_ref.1, f32[768]{0:T(1024)} %bias_ref.1, f32[16,768]{1,0:T(8,128)} %a_log_ref.1, ...), custom_call_target="tpu_custom_call" | custom-call | tf_op jit(solution)/shard_map/pallas_call | solution.py:431
  57.2 1.7 %copy.13 = bf16[12,12,768]{2,1,0:T(8,128)(2,1)} copy(bf16[12,12,768]{2,1,0:T(8,128)(2,1)} %get-tuple-element.4) | data formatting | bytes 442368
  58.9 1.7 %copy.14 = bf16[12,12,768]{2,1,0:T(8,128)(2,1)} copy(bf16[12,12,768]{2,1,0:T(8,128)(2,1)} %get-tuple-element.5) | data formatting | bytes 442368

commit v6 on v5

--- a/solution.py
+++ b/solution.py
@@ -11,7 +11,7 @@
 MESH = pl.DeviceIdType.MESH
 LANES = 128
 BLOCK = 256
-START, LOCAL, COL_HOP, ROW_HOP, SPACE, NEVER = 1000, 1500, 2500, 3000, 2000, 1 << 30
+START, LOCAL, COL_HOP, ROW_HOP, SPACE, LATER, NEVER = 1000, 1500, 2500, 3000, 2000, 4000, 1 << 30
 F32 = jnp.float32
 BF16 = jnp.bfloat16
 
@@ -243,7 +243,7 @@
             e1r[k, i] = state
             return tuple(after)
 
-        terms = lax.fori_loop(0, tr, line, (zero,) * tc, unroll=2)
+        terms = lax.fori_loop(0, tr, line, (zero,) * tc)
         for j in range(tc):
             e1c[k, j] = terms[j]
         head_send(0, k)
@@ -264,7 +264,7 @@
                 after.append(d * states_in[j] + state)
             return tuple(after)
 
-        ends = lax.fori_loop(0, tr, down_line, (zero,) * tc, unroll=2)
+        ends = lax.fori_loop(0, tr, down_line, (zero,) * tc)
         for j in range(tc):
             e2c[k, j] = ends[j]
         head_send(2, k)
@@ -287,7 +287,7 @@
             e2r[k, i] = term
             return tuple(after)
 
-        lax.fori_loop(0, tr, up_line, tuple(in1c[k, j] for j in range(tc)), unroll=2)
+        lax.fori_loop(0, tr, up_line, tuple(in1c[k, j] for j in range(tc)))
         head_send(3, k)
 
     def col_link(k):
@@ -325,7 +325,7 @@
                 cacc_row[cell(j)] += full * g_ref[i, j : j + 1, cut]
             return carry
 
-        lax.fori_loop(0, tr, last_line, 0, unroll=2)
+        lax.fori_loop(0, tr, last_line, 0)
 
     below, after = (n_row - 1 - r) // 2, (n_col - 1 - p) // 2
 
@@ -338,10 +338,12 @@
     table = (
         (local_ends, lambda k: START * k),
         (row_step, lambda k: START + 1 + COL_HOP * (p // 2) + START * k),
-        (col_step, lambda k: START + 1 + ROW_HOP * below + SPACE * k),
+        (col_step, lambda k: START + 1 + ROW_HOP * below + START * k),
         (col_link, col_time),
         (row_link, row_time),
-        (finish, lambda k: jnp.maximum(col_time(k), row_time(k)) + 1),
+        (finish, lambda k: 1 + jnp.maximum(
+            col_time(k) + jnp.where(last_row, 0, LATER), row_time(k) + jnp.where(first_col, 0, LATER)
+        )),
     )
 
     def slot(_, counts):

time: 60.8 us -> 63.3 us (1.041)
  Pallas kernels: 56.6 us -> 59.1 us
    pallas_call x1, Pallas kernels: 56.6 us -> 59.1 us  [body(): pl.pallas_call(functools.partial(layer_kernel, sizes), out_shape=(out, ou...]
where the time goes in v6:
time: 63.3 us; the launch traced here: 63.1 us
  Pallas kernels  59.1 us (93%)
  local copies, waits for them, and re-layouts  3.39 us (5%)
  between operations  0.64 us (1%)
    pallas_call x1, Pallas kernels, body(): pl.pallas_call(functools.partial(layer_kernel, sizes), out_shape=(out, ou...  59.1 us
    unnamed x2, local copies, waits for them, and re-layouts  3.39 us

profile of v6, /device:TPU:0, one launch (start us, length us, event | category | flops | bytes accessed | tf_op | source)
XLA Modules:
  0.0 63.1 jit_solution(16085695866223125751)
XLA Ops:
  0.6 59.1 %shard_map.104 = (bf16[12,12,768]{2,1,0:T(8,128)(2,1)}, bf16[12,12,768]{2,1,0:T(8,128)(2,1)}) custom-call(bf16[12,12,768]{2,1,0:T(8,128)(2,1)} %tokens_ref.1, bf16[768,1536]{1,0:T(8,128)(2,1)} %w_in_ref.1, bf16[80,768]{1,0:T(8,128)(2,1)} %bitcast.1, bf16[48,768]{1,0:T(8,128)(2,1)} %w_dt_ref.1, f32[768]{0:T(1024)} %bias_ref.1, f32[16,768]{1,0:T(8,128)} %a_log_ref.1, ...), custom_call_target="tpu_custom_call" | custom-call | tf_op jit(solution)/shard_map/pallas_call | solution.py:433
  59.8 1.7 %copy.13 = bf16[12,12,768]{2,1,0:T(8,128)(2,1)} copy(bf16[12,12,768]{2,1,0:T(8,128)(2,1)} %get-tuple-element.4) | data formatting | bytes 442368
  61.4 1.7 %copy.14 = bf16[12,12,768]{2,1,0:T(8,128)(2,1)} copy(bf16[12,12,768]{2,1,0:T(8,128)(2,1)} %get-tuple-element.5) | data formatting | bytes 442368

commit v7 on v6

--- a/solution.py
+++ b/solution.py
@@ -11,13 +11,13 @@
 MESH = pl.DeviceIdType.MESH
 LANES = 128
 BLOCK = 256
-START, LOCAL, COL_HOP, ROW_HOP, SPACE, LATER, NEVER = 1000, 1500, 2500, 3000, 2000, 4000, 1 << 30
+START, LOCAL, COL_HOP, ROW_HOP, SPACE, NEVER = 1000, 1500, 2500, 3000, 2000, 1 << 30
 F32 = jnp.float32
 BF16 = jnp.bfloat16
 
 
 def sigmoid(values):
-    return 1.0 / (1.0 + jnp.exp(-values))
+    return 0.5 + 0.5 * jnp.tanh(0.5 * values)
 
 
 def silu_grad(values):
@@ -338,12 +338,10 @@
     table = (
         (local_ends, lambda k: START * k),
         (row_step, lambda k: START + 1 + COL_HOP * (p // 2) + START * k),
-        (col_step, lambda k: START + 1 + ROW_HOP * below + START * k),
+        (col_step, lambda k: START + 1 + ROW_HOP * below + SPACE * k),
         (col_link, col_time),
         (row_link, row_time),
-        (finish, lambda k: 1 + jnp.maximum(
-            col_time(k) + jnp.where(last_row, 0, LATER), row_time(k) + jnp.where(first_col, 0, LATER)
-        )),
+        (finish, lambda k: jnp.maximum(col_time(k), row_time(k)) + 1),
     )
 
     def slot(_, counts):
@@ -380,7 +378,7 @@
             get(gated_ref, cut) * scan_out * silu_grad(z_pre))
         step_grad = get(sd_ref, cut) * math.log(2.0) + get(rb_ref, cut) * x
         low_grad = low_grad + dot_transposed(
-            (step_grad * sigmoid(dt_pre)).astype(BF16), w_dt_ref[:, cut]
+            (step_grad / (1.0 + jnp.exp(-dt_pre))).astype(BF16), w_dt_ref[:, cut]
         )
     layer_ref[...] = layer.reshape(tr, pad, model)[:, :tc, :].astype(BF16)
     xd_ref[:, :rank] = low_grad

time: 63.3 us -> 61.6 us (0.973)
  Pallas kernels: 59.1 us -> 57.4 us
    pallas_call x1, Pallas kernels: 59.1 us -> 57.4 us  [body(): pl.pallas_call(functools.partial(layer_kernel, sizes), out_shape=(out, ou...]
where the time goes in v7:
time: 61.6 us; the launch traced here: 61.4 us
  Pallas kernels  57.4 us (93%)
  local copies, waits for them, and re-layouts  3.39 us (6%)
  between operations  0.64 us (1%)
    pallas_call x1, Pallas kernels, body(): pl.pallas_call(functools.partial(layer_kernel, sizes), out_shape=(out, ou...  57.4 us
    unnamed x2, local copies, waits for them, and re-layouts  3.39 us

profile of v7, /device:TPU:0, one launch (start us, length us, event | category | flops | bytes accessed | tf_op | source)
XLA Modules:
  0.0 61.4 jit_solution(2437665431268573430)
XLA Ops:
  0.6 57.4 %shard_map.104 = (bf16[12,12,768]{2,1,0:T(8,128)(2,1)}, bf16[12,12,768]{2,1,0:T(8,128)(2,1)}) custom-call(bf16[12,12,768]{2,1,0:T(8,128)(2,1)} %tokens_ref.1, bf16[768,1536]{1,0:T(8,128)(2,1)} %w_in_ref.1, bf16[80,768]{1,0:T(8,128)(2,1)} %bitcast.1, bf16[48,768]{1,0:T(8,128)(2,1)} %w_dt_ref.1, f32[768]{0:T(1024)} %bias_ref.1, f32[16,768]{1,0:T(8,128)} %a_log_ref.1, ...), custom_call_target="tpu_custom_call" | custom-call | tf_op jit(solution)/shard_map/pallas_call | solution.py:431
  58.0 1.7 %copy.13 = bf16[12,12,768]{2,1,0:T(8,128)(2,1)} copy(bf16[12,12,768]{2,1,0:T(8,128)(2,1)} %get-tuple-element.4) | data formatting | bytes 442368
  59.7 1.7 %copy.14 = bf16[12,12,768]{2,1,0:T(8,128)(2,1)} copy(bf16[12,12,768]{2,1,0:T(8,128)(2,1)} %get-tuple-element.5) | data formatting | bytes 442368
